TPU v7x, 128 devices: a whole 4x4x4 slice. The times are simulated.
128 devices in a mesh: grp: 128 (over z, y, x, core).
Axes of the slice: x: 4, y: 4, z: 4, core: 2. Of those that a mesh axis runs over, the one named last changes fastest.
Arguments:
- right_side: float32 [384, 256, 2048], P('grp'), may hold values from -12 to 12
- fine_smoother: float32 [1, 256, 256], replicated, may hold values from -0.1 to 0.1
- level_two_smoother: float32 [128, 128], replicated, may hold values from -0.25 to 0.25
- level_three_smoother: float32 [64, 64], replicated, may hold values from -0.25 to 0.25
- level_four_smoother: float32 [32, 32], replicated, may hold values from -0.25 to 0.25
Outputs:
- solution: float32 [384, 256, 2048], P('grp')
- pending_correction: float32 [384, 256, 2048], P('grp')
All inputs are finite; a program needn't handle non-finite values.
Results may differ from a plain program's by a relative error of at most 0.0003.
Values sent between devices are 32-bit elements; how exact they have to be, the bound alone decides.
A program may use at most 192 MiB of HBM per device.

v0:
```python
import jax
import jax.numpy as jnp
from jax import lax
from jax.experimental import pallas as pl
from jax.experimental.pallas import tpu as pltpu
from jax.sharding import PartitionSpec as P

MESH = pl.DeviceIdType.MESH
F32 = jnp.float32
BF16 = jnp.bfloat16

FINE_Z = 4.0
LANES = 128
AHEAD = 3
LAG = 4
ROWS = 64


def parts_of(m):
    head = m.astype(BF16)
    rest = m - head.astype(F32)
    middle = rest.astype(BF16)
    return head, middle, (rest - middle.astype(F32)).astype(BF16)


def exact_dot(a, b):
    a1, a2, a3 = parts_of(a)
    b1, b2, b3 = parts_of(b)
    left = jnp.concatenate([a1, a1, a2, a1, a2, a3], axis=1)
    right = jnp.concatenate([b1, b2, b1, b3, b2, b1], axis=0)
    return jnp.dot(left, right, preferred_element_type=F32)


def second_difference(m):
    order = m.shape[0]
    row = lax.broadcasted_iota(jnp.int32, m.shape, 0)
    below = jnp.where(row == 0, 0.0, pltpu.roll(m, 1, 0))
    above = jnp.where(row == order - 1, 0.0, pltpu.roll(m, order - 1, 0))
    return 2.0 * m - below - above


def line_pair(m, vertical):
    square = exact_dot(m, m)
    mixed = exact_dot(m, second_difference(m))
    return 2.0 * m - vertical * mixed - 4.0 * square, square


def spread(rows, columns, factor):
    row = lax.broadcasted_iota(jnp.int32, (rows, columns), 0)
    column = lax.broadcasted_iota(jnp.int32, (rows, columns), 1)
    return ((row >= factor * column) & (row < factor * column + factor)).astype(F32)


def gather(rows, columns, factor):
    row = lax.broadcasted_iota(jnp.int32, (rows, columns), 0)
    column = lax.broadcasted_iota(jnp.int32, (rows, columns), 1)
    return ((column >= factor * row) & (column < factor * row + factor)).astype(F32)


def build_terms(fine, two, three, four, coarse, left_terms, right_terms, product, totals, doubled, terms):
    nz = fine.shape[0]
    half = nz // 2
    p0, q = line_pair(fine, FINE_Z)

    def scaled(m):
        return 4.0 * m + FINE_Z * second_difference(m)

    row = lax.broadcasted_iota(jnp.int32, (nz, nz), 0)
    column = lax.broadcasted_iota(jnp.int32, (nz, nz), 1)
    left_terms[0:nz] = p0
    left_terms[nz : 2 * nz] = q
    right_terms[0] = (row == column).astype(F32) - scaled(p0)
    right_terms[1] = p0 - scaled(q)
    right_terms[2] = q

    c0, c1 = line_pair(two, FINE_Z / 4.0)
    for m, factor, vertical in ((three, 2, FINE_Z / 16.0), (four, 4, FINE_Z / 64.0)):
        up, down = spread(half, half, factor), gather(half, half, factor)
        wide = exact_dot(up, jnp.concatenate(line_pair(m, vertical), axis=1))
        coarse[0:half] = wide[:, 0:half]
        coarse[half:nz] = wide[:, half:nz]
        both = exact_dot(coarse[...], down)
        c0 = c0 + both[0:half]
        c1 = c1 + both[half:nz]
    coarse[0:half] = c0
    coarse[half:nz] = c1
    both = exact_dot(coarse[...], gather(half, nz, 2))
    left_terms[2 * nz : 3 * nz] = both
    for k, base in ((0, p0), (1, q)):
        for h in range(nz // LANES):
            columns = slice(h * LANES, (h + 1) * LANES)
            part = left_terms[2 * nz + k * half : 2 * nz + (k + 1) * half, columns]
            for side in range(2):
                doubled[h, pl.ds(side, half, stride=2)] = part
            totals[k, 0:nz, columns] = base[:, columns] + doubled[h]
    for k in range(4):
        if k >= 2:
            totals[k, 0:nz] = jnp.zeros((nz, nz), F32)
        totals[k, nz : nz + half] = jnp.zeros((half, nz), F32)
    for j in range(3):
        product[...] = exact_dot(left_terms[...], right_terms[j])
        totals[j, 0:nz] += product[0:nz]
        totals[j + 1, 0:nz] += product[nz : 2 * nz]
        totals[j, nz : nz + half] += product[2 * nz : 2 * nz + half]
        totals[j + 1, nz : nz + half] += product[2 * nz + half : 3 * nz]
    for k in range(4):
        total = totals[k]
        head = total.astype(BF16)
        terms[k, :, 0:nz] = head
        terms[k, :, nz : 2 * nz] = head
        terms[k, :, 2 * nz : 3 * nz] = (total - head.astype(F32)).astype(BF16)


def stacked(planes):
    cells = jnp.concatenate(planes, axis=1)
    head = cells.astype(BF16)
    tail = (cells - head.astype(F32)).astype(BF16)
    return jnp.concatenate([head, tail, head], axis=0)


def kernel(
    count,
    right_side, fine, two, three, four,
    sol, pend,
    own, near_l, near_r, far_l, far_r,
    v3, v2, v1, v0,
    fine_v, two_v, three_v, four_v, left_terms, right_terms, product, totals, terms, doubled, padded, coarse,
    own_sem, small_sem, near_send, near_recv, far_send, far_recv,
):
    me = lax.axis_index("grp")
    has_l, has_r = me > 0, me < count - 1
    chunks = own.shape[0]
    rows = v0.shape[2]
    nz = own.shape[2]

    barrier = pltpu.get_barrier_semaphore()

    @pl.when(has_l)
    def _():
        pl.semaphore_signal(barrier, inc=1, device_id=(me - 1,), device_id_type=MESH)

    @pl.when(has_r)
    def _():
        pl.semaphore_signal(barrier, inc=1, device_id=(me + 1,), device_id_type=MESH)

    pl.semaphore_wait(barrier, has_l.astype(jnp.int32) + has_r.astype(jnp.int32))

    def cut(c):
        return pl.ds(pl.multiple_of(c * LANES, LANES), LANES)

    def remote(planes, buffer, sends, recvs, way, c, target):
        return pltpu.make_async_remote_copy(
            src_ref=right_side.at[planes, :, cut(c)],
            dst_ref=buffer.at[c],
            send_sem=sends.at[way, c],
            recv_sem=recvs.at[way, c],
            device_id=(target,),
            device_id_type=MESH,
        )

    def near_left(c):
        return remote(pl.ds(0, 2), near_r, near_send, near_recv, 0, c, me - 1)

    def near_right(c):
        return remote(pl.ds(1, 2), near_l, near_send, near_recv, 1, c, me + 1)

    def far_left(c):
        return remote(2, far_r, far_send, far_recv, 0, c, me - 1)

    def far_right(c):
        return remote(0, far_l, far_send, far_recv, 1, c, me + 1)

    def start(to_left, to_right, c):
        @pl.when(has_l)
        def _():
            to_left(c).start()

        @pl.when(has_r)
        def _():
            to_right(c).start()

    def finish(to_left, to_right, c):
        @pl.when(has_l)
        def _():
            to_left(c).wait_send()
            to_right(c).wait_recv()

        @pl.when(has_r)
        def _():
            to_right(c).wait_send()
            to_left(c).wait_recv()

    for c in range(AHEAD):
        start(near_left, near_right, c)

    small = [
        pltpu.make_async_copy(src, dst, small_sem.at[i])
        for i, (src, dst) in enumerate(
            ((fine.at[0], fine_v), (two, two_v), (three, three_v), (four, four_v))
        )
    ]
    for copy in small:
        copy.start()

    def own_copy(c):
        return pltpu.make_async_copy(right_side.at[:, :, cut(c)], own.at[c], own_sem.at[c])

    lax.fori_loop(0, chunks, lambda c, _: (own_copy(c).start(), 0)[1], 0)

    plane = jnp.zeros((rows, LANES), F32)
    for ring in (v3, v2, v1):
        for p in range(ring.shape[1]):
            ring[ring.shape[0] - 1, p] = plane
    for slot in range(v3.shape[0]):
        v3[slot, 0] = plane
        v3[slot, v3.shape[1] - 1] = plane

    def clear(near, far):
        def body(c, _):
            near[c] = jnp.zeros(near.shape[1:], F32)
            far[c] = jnp.zeros(far.shape[1:], F32)
            return 0

        lax.fori_loop(0, chunks, body, 0)

    @pl.when(jnp.logical_not(has_l))
    def _():
        clear(near_l, far_l)

    @pl.when(jnp.logical_not(has_r))
    def _():
        clear(near_r, far_r)

    for copy in small:
        copy.wait()
    for i, m in enumerate((three_v, four_v)):
        order = m.shape[0]
        padded[i] = jnp.zeros(padded.shape[1:], F32)
        padded[i, 0:order, 0:order] = m[...]
    build_terms(fine_v[...], two_v[...], padded[0], padded[1], coarse,
        left_terms, right_terms, product, totals, doubled, terms)

    def slot(ring, c):
        return lax.rem(c, ring.shape[0])

    def spread_out(c):
        s3, s2, s1, s0 = slot(v3, c), slot(v2, c), slot(v1, c), slot(v0, c)
        rings = {3: (v3, s3, 3), 2: (v2, s2, 2), 1: (v1, s1, 1), 0: (v0, s0, 0)}

        def apply(places, planes, orders):
            source = stacked(planes)
            for k in orders:
                ring, s, offset = rings[k]
                product = jnp.dot(terms[k], source, preferred_element_type=F32)
                for i, x in enumerate(places):
                    ring[s, x + offset] = product[:, i * LANES : (i + 1) * LANES]

        apply((0, 1, 2), [own[c, 0], own[c, 1], own[c, 2]], (3, 2, 1, 0))
        apply((-1, 3), [near_l[c, 1], near_r[c, 0]], (3, 2, 1))
        apply((-2, 4), [near_l[c, 0], near_r[c, 1]], (3, 2))

    lane = lax.broadcasted_iota(jnp.int32, (ROWS, LANES), 1)
    first_lane, last_lane = lane == 0, lane == LANES - 1

    def neighbours(source, target, shift, lo, hi, t):
        before, here, after = slot(source, t + source.shape[0] - 1), slot(source, t), slot(source, t + 1)
        into = slot(target, t)

        def body(p, _):
            q = p + shift
            for b in range(rows // ROWS):
                part = pl.ds(b * ROWS, ROWS)
                centre = source[here, q, part]
                up = pltpu.roll(jnp.where(first_lane, source[after, q, part], centre), LANES - 1, 1)
                down = pltpu.roll(jnp.where(last_lane, source[before, q, part], centre), 1, 1)
                beside = source[here, q - 1, part] + source[here, q + 1, part]
                target[into, p, part] = target[into, p, part] + (beside + (up + down))
            return 0

        lax.fori_loop(lo, hi, body, 0)

    skip_l = jnp.where(has_l, 0, 1)
    skip_r = jnp.where(has_r, 0, 1)

    def add_far(j):
        source = stacked([far_l[j], far_r[j]])
        product = jnp.dot(terms[3], source, preferred_element_type=F32)
        s = slot(v0, j)
        columns = cut(j)
        for p in range(3):
            total = v0[s, p]
            if p == 0:
                total = total + product[:, 0:LANES]
            if p == 2:
                total = total + product[:, LANES : 2 * LANES]
            sol[p, :, columns] = total[0:nz]
            for side in range(2):
                doubled[p, pl.ds(side, nz // 2, stride=2)] = total[nz:rows]
            pend[p, :, columns] = doubled[p]

    def zero_slot(ring, c):
        def body(p, _):
            ring[slot(ring, c), p] = jnp.zeros((rows, LANES), F32)
            return 0

        lax.fori_loop(0, ring.shape[1], body, 0)

    def step(c, _):
        @pl.when(c < chunks)
        def _():
            own_copy(c).wait()
            finish(near_left, near_right, c)

        @pl.when(c + AHEAD < chunks)
        def _():
            start(near_left, near_right, c + AHEAD)

            @pl.when(c + AHEAD >= LAG)
            def _():
                start(far_left, far_right, c + AHEAD - LAG)

        @pl.when(c + AHEAD == chunks)
        def _():
            for i in range(LAG):
                start(far_left, far_right, chunks - LAG + i)

        @pl.when(c < chunks)
        def _():
            spread_out(c)

        @pl.when(c == chunks)
        def _():
            zero_slot(v3, chunks)

        @pl.when((c >= 1) & (c < chunks + 1))
        def _():
            neighbours(v3, v2, 1, 2 * skip_l, 7 - 2 * skip_r, c - 1)

        @pl.when(c == chunks + 1)
        def _():
            zero_slot(v2, chunks)

        @pl.when((c >= 2) & (c < chunks + 2))
        def _():
            neighbours(v2, v1, 1, skip_l, 5 - skip_r, c - 2)

        @pl.when(c == chunks + 2)
        def _():
            zero_slot(v1, chunks)

        @pl.when((c >= 3) & (c < chunks + 3))
        def _():
            neighbours(v1, v0, 1, 0, 3, c - 3)

        @pl.when(c >= LAG)
        def _():
            finish(far_left, far_right, c - LAG)
            add_far(c - LAG)

        return 0

    lax.fori_loop(0, chunks + LAG, step, 0)


def put_out(sol, pend, sol_out, pend_out, sems):
    copies = []
    for p in range(sol.shape[0]):
        copies.append(pltpu.make_async_copy(sol.at[p], sol_out.at[p], sems.at[0, p]))
        copies.append(pltpu.make_async_copy(pend.at[p], pend_out.at[p], sems.at[1, p]))
    for copy in copies:
        copy.start()
    for copy in copies:
        copy.wait()


def solution(mesh):
    count = mesh.shape["grp"]
    anywhere = pl.BlockSpec(memory_space=pl.ANY)
    vmem = pl.BlockSpec(memory_space=pltpu.VMEM)

    def per_device(right_side, fine, two, three, four):
        planes, nz, ny = right_side.shape
        chunks = ny // LANES
        rows = nz + nz // 2
        shape = (planes, nz, ny)

        def body(*refs):
            kernel(count, *refs)

        sol, pend = pl.pallas_call(
            body,
            out_shape=(pltpu.VMEM(shape, F32), pltpu.VMEM(shape, F32)),
            in_specs=[anywhere] * 5,
            out_specs=(vmem, vmem),
            scratch_shapes=[
                pltpu.VMEM((chunks, planes, nz, LANES), F32),
                pltpu.VMEM((chunks, 2, nz, LANES), F32),
                pltpu.VMEM((chunks, 2, nz, LANES), F32),
                pltpu.VMEM((chunks, nz, LANES), F32),
                pltpu.VMEM((chunks, nz, LANES), F32),
                pltpu.VMEM((3, planes + 6, rows, LANES), F32),
                pltpu.VMEM((4, planes + 4, rows, LANES), F32),
                pltpu.VMEM((5, planes + 2, rows, LANES), F32),
                pltpu.VMEM((5, planes, rows, LANES), F32),
                pltpu.VMEM(fine.shape[1:], F32),
                pltpu.VMEM(two.shape, F32),
                pltpu.VMEM(three.shape, F32),
                pltpu.VMEM(four.shape, F32),
                pltpu.VMEM((3 * nz, nz), F32),
                pltpu.VMEM((3, nz, nz), F32),
                pltpu.VMEM((3 * nz, nz), F32),
                pltpu.VMEM((4, rows, nz), F32),
                pltpu.VMEM((4, rows, 3 * nz), BF16),
                pltpu.VMEM((planes, nz, LANES), F32),
                pltpu.VMEM((2, nz // 2, nz // 2), F32),
                pltpu.VMEM((nz, nz // 2), F32),
                pltpu.SemaphoreType.DMA((chunks,)),
                pltpu.SemaphoreType.DMA((4,)),
                pltpu.SemaphoreType.DMA((2, chunks)),
                pltpu.SemaphoreType.DMA((2, chunks)),
                pltpu.SemaphoreType.DMA((2, chunks)),
                pltpu.SemaphoreType.DMA((2, chunks)),
            ],
            compiler_params=pltpu.CompilerParams(
                collective_id=1, has_side_effects=True, vmem_limit_bytes=50 << 20
            ),
        )(right_side, fine, two, three, four)
        sol = pltpu.with_memory_space_constraint(sol, pltpu.VMEM)
        pend = pltpu.with_memory_space_constraint(pend, pltpu.VMEM)
        return pl.pallas_call(
            put_out,
            out_shape=(jax.ShapeDtypeStruct(shape, F32), jax.ShapeDtypeStruct(shape, F32)),
            in_specs=[vmem, vmem],
            out_specs=(anywhere, anywhere),
            scratch_shapes=[pltpu.SemaphoreType.DMA((2, planes))],
            compiler_params=pltpu.CompilerParams(vmem_limit_bytes=16 << 20),
        )(sol, pend)

    in_specs = (P("grp", None, None), P(), P(), P(), P())
    out_specs = (P("grp", None, None), P("grp", None, None))
    return jax.shard_map(
        per_device, mesh=mesh, in_specs=in_specs, out_specs=out_specs, check_vma=False
    )
```

profile of v0, /device:TPU:31, one launch (start us, length us, event | category | flops | bytes accessed | tf_op | source)
XLA Modules:
  0.0 101.2 jit_solution(5666652496895286015)
XLA Ops:
  0.6 95.9 %shard_map.68 = (f32[3,256,2048]{2,1,0:T(8,128)S(1)}, f32[3,256,2048]{2,1,0:T(8,128)S(1)}) custom-call(f32[3,256,2048]{2,1,0:T(8,128)} %refs_0_.1, f32[1,256,256]{2,1,0:T(8,128)} %refs_1_.1, f32[128,128]{1,0:T(8,128)} %refs_2_.1, f32[64,64]{1,0:T(8,128)} %refs_3_.1, f32[32,32]{1,0:T(8,128)} %refs_4_.1), custom_call_target="tpu_custom_call" | custom-call | tf_op jit(solution)/shard_map/pallas_call | solution.py:390
  96.5 4.6 %shard_map.69 = (f32[3,256,2048]{2,1,0:T(8,128)}, f32[3,256,2048]{2,1,0:T(8,128)}) custom-call(f32[3,256,2048]{2,1,0:T(8,128)S(1)} %get-tuple-element.4.sol, f32[3,256,2048]{2,1,0:T(8,128)S(1)} %get-tuple-element.5.pend), custom_call_target="tpu_custom_call" | custom-call | tf_op jit(solution)/shard_map/pallas_call | solution.py:430
where the time goes:
time: 101 us
  Pallas kernels  101 us (100%)
    pallas_call x1, Pallas kernels, per_device(): pl.pallas_call(body, out_shape=(pltpu.VMEM(shape, F32), pltpu.VMEM(shape,...  95.9 us
    pallas_call x1, Pallas kernels, per_device(): pl.pallas_call(put_out, out_shape=(jax.ShapeDtypeStruct(shape, F32), jax....  4.65 us

commit v1 on v0

--- a/solution.py
+++ b/solution.py
@@ -12,8 +12,8 @@
 FINE_Z = 4.0
 LANES = 128
 AHEAD = 3
-LAG = 4
-ROWS = 64
+LAG = 6
+ROWS = 32
 
 
 def parts_of(m):
@@ -105,33 +105,38 @@
         totals[j + 1, nz : nz + half] += product[2 * nz + half : 3 * nz]
     for k in range(4):
         total = totals[k]
+        columns = slice(k * nz, (k + 1) * nz)
         head = total.astype(BF16)
-        terms[k, :, 0:nz] = head
-        terms[k, :, nz : 2 * nz] = head
-        terms[k, :, 2 * nz : 3 * nz] = (total - head.astype(F32)).astype(BF16)
-
-
-def stacked(planes):
-    cells = jnp.concatenate(planes, axis=1)
+        terms[0 : nz + half, columns] = head
+        terms[nz + half :, columns] = (total - head.astype(F32)).astype(BF16)
+
+
+def halves(cells):
     head = cells.astype(BF16)
-    tail = (cells - head.astype(F32)).astype(BF16)
-    return jnp.concatenate([head, tail, head], axis=0)
+    return head, (cells - head.astype(F32)).astype(BF16)
+
+
+def product_of(terms, columns, head, tail):
+    rows = terms.shape[0] // 2
+    both = jnp.dot(terms[:, columns], head, preferred_element_type=F32)
+    rest = jnp.dot(terms[0:rows, columns], tail, preferred_element_type=F32)
+    return both[0:rows] + (both[rows:] + rest)
 
 
 def kernel(
     count,
     right_side, fine, two, three, four,
     sol, pend,
-    own, near_l, near_r, far_l, far_r,
-    v3, v2, v1, v0,
+    cells, far_l, far_r,
+    once, twice, head, tail, sums,
     fine_v, two_v, three_v, four_v, left_terms, right_terms, product, totals, terms, doubled, padded, coarse,
     own_sem, small_sem, near_send, near_recv, far_send, far_recv,
 ):
     me = lax.axis_index("grp")
     has_l, has_r = me > 0, me < count - 1
-    chunks = own.shape[0]
-    rows = v0.shape[2]
-    nz = own.shape[2]
+    chunks = far_l.shape[0]
+    rows = sums.shape[2]
+    nz = cells.shape[2]
 
     barrier = pltpu.get_barrier_semaphore()
 
@@ -148,27 +153,29 @@
     def cut(c):
         return pl.ds(pl.multiple_of(c * LANES, LANES), LANES)
 
-    def remote(planes, buffer, sends, recvs, way, c, target):
+    def remote(planes, target, sends, recvs, way, c, device):
         return pltpu.make_async_remote_copy(
             src_ref=right_side.at[planes, :, cut(c)],
-            dst_ref=buffer.at[c],
+            dst_ref=target,
             send_sem=sends.at[way, c],
             recv_sem=recvs.at[way, c],
-            device_id=(target,),
+            device_id=(device,),
             device_id_type=MESH,
         )
 
     def near_left(c):
-        return remote(pl.ds(0, 2), near_r, near_send, near_recv, 0, c, me - 1)
+        target = cells.at[c + 1, pl.ds(5, 2)]
+        return remote(pl.ds(0, 2), target, near_send, near_recv, 0, c, me - 1)
 
     def near_right(c):
-        return remote(pl.ds(1, 2), near_l, near_send, near_recv, 1, c, me + 1)
+        target = cells.at[c + 1, pl.ds(0, 2)]
+        return remote(pl.ds(1, 2), target, near_send, near_recv, 1, c, me + 1)
 
     def far_left(c):
-        return remote(2, far_r, far_send, far_recv, 0, c, me - 1)
+        return remote(2, far_r.at[c], far_send, far_recv, 0, c, me - 1)
 
     def far_right(c):
-        return remote(0, far_l, far_send, far_recv, 1, c, me + 1)
+        return remote(0, far_l.at[c], far_send, far_recv, 1, c, me + 1)
 
     def start(to_left, to_right, c):
         @pl.when(has_l)
@@ -203,33 +210,41 @@
         copy.start()
 
     def own_copy(c):
-        return pltpu.make_async_copy(right_side.at[:, :, cut(c)], own.at[c], own_sem.at[c])
+        return pltpu.make_async_copy(
+            right_side.at[:, :, cut(c)], cells.at[c + 1, pl.ds(2, 3)], own_sem.at[c]
+        )
 
     lax.fori_loop(0, chunks, lambda c, _: (own_copy(c).start(), 0)[1], 0)
 
-    plane = jnp.zeros((rows, LANES), F32)
-    for ring in (v3, v2, v1):
-        for p in range(ring.shape[1]):
-            ring[ring.shape[0] - 1, p] = plane
-    for slot in range(v3.shape[0]):
-        v3[slot, 0] = plane
-        v3[slot, v3.shape[1] - 1] = plane
-
-    def clear(near, far):
-        def body(c, _):
-            near[c] = jnp.zeros(near.shape[1:], F32)
-            far[c] = jnp.zeros(far.shape[1:], F32)
-            return 0
-
-        lax.fori_loop(0, chunks, body, 0)
+    plane = jnp.zeros((nz, LANES), F32)
+    for p in range(7):
+        cells[0, p] = plane
+        cells[chunks + 1, p] = plane
+
+    def clear(ring, s, planes):
+        for p in planes:
+            ring[s, p] = plane
+
+    clear(once, once.shape[0] - 1, range(7))
+    clear(twice, twice.shape[0] - 1, range(5))
 
     @pl.when(jnp.logical_not(has_l))
     def _():
-        clear(near_l, far_l)
+        def body(c, _):
+            clear(cells, c + 1, range(0, 2))
+            far_l[c] = plane
+            return 0
+
+        lax.fori_loop(0, chunks, body, 0)
 
     @pl.when(jnp.logical_not(has_r))
     def _():
-        clear(near_r, far_r)
+        def body(c, _):
+            clear(cells, c + 1, range(5, 7))
+            far_r[c] = plane
+            return 0
+
+        lax.fori_loop(0, chunks, body, 0)
 
     for copy in small:
         copy.wait()
@@ -243,52 +258,84 @@
     def slot(ring, c):
         return lax.rem(c, ring.shape[0])
 
-    def spread_out(c):
-        s3, s2, s1, s0 = slot(v3, c), slot(v2, c), slot(v1, c), slot(v0, c)
-        rings = {3: (v3, s3, 3), 2: (v2, s2, 2), 1: (v1, s1, 1), 0: (v0, s0, 0)}
-
-        def apply(places, planes, orders):
-            source = stacked(planes)
-            for k in orders:
-                ring, s, offset = rings[k]
-                product = jnp.dot(terms[k], source, preferred_element_type=F32)
-                for i, x in enumerate(places):
-                    ring[s, x + offset] = product[:, i * LANES : (i + 1) * LANES]
-
-        apply((0, 1, 2), [own[c, 0], own[c, 1], own[c, 2]], (3, 2, 1, 0))
-        apply((-1, 3), [near_l[c, 1], near_r[c, 0]], (3, 2, 1))
-        apply((-2, 4), [near_l[c, 0], near_r[c, 1]], (3, 2))
-
     lane = lax.broadcasted_iota(jnp.int32, (ROWS, LANES), 1)
     first_lane, last_lane = lane == 0, lane == LANES - 1
 
-    def neighbours(source, target, shift, lo, hi, t):
-        before, here, after = slot(source, t + source.shape[0] - 1), slot(source, t), slot(source, t + 1)
-        into = slot(target, t)
-
-        def body(p, _):
-            q = p + shift
-            for b in range(rows // ROWS):
-                part = pl.ds(b * ROWS, ROWS)
-                centre = source[here, q, part]
-                up = pltpu.roll(jnp.where(first_lane, source[after, q, part], centre), LANES - 1, 1)
-                down = pltpu.roll(jnp.where(last_lane, source[before, q, part], centre), 1, 1)
-                beside = source[here, q - 1, part] + source[here, q + 1, part]
-                target[into, p, part] = target[into, p, part] + (beside + (up + down))
-            return 0
-
-        lax.fori_loop(lo, hi, body, 0)
-
-    skip_l = jnp.where(has_l, 0, 1)
-    skip_r = jnp.where(has_r, 0, 1)
+    def neighbour_sum(source, slots, targets, put):
+        before, here, after = slots
+        for b in range(nz // ROWS):
+            part = pl.ds(b * ROWS, ROWS)
+            centres = [source[here, q, part] for q in range(source.shape[1])]
+            for p, q in targets:
+                up = jnp.where(first_lane, source[after, q, part], centres[q])
+                down = jnp.where(last_lane, source[before, q, part], centres[q])
+                total = pltpu.roll(up, LANES - 1, 1) + pltpu.roll(down, 1, 1)
+                for x in (q - 1, q + 1):
+                    if 0 <= x < len(centres):
+                        total = total + centres[x]
+                put(p, part, total)
+
+    def around(ring, c):
+        size = ring.shape[0]
+        return tuple(lax.rem(c + size + i, size) for i in (-1, 0, 1))
+
+    def first_sum(c):
+        s = slot(once, c)
+
+        def put(p, part, total):
+            once[s, p, part] = total
+
+        neighbour_sum(cells, (c, c + 1, c + 2), [(p, p) for p in range(7)], put)
+
+        @pl.when(jnp.logical_not(has_l))
+        def _():
+            clear(once, s, range(0, 2))
+
+        @pl.when(jnp.logical_not(has_r))
+        def _():
+            clear(once, s, range(5, 7))
+
+    def second_sum(c):
+        s = slot(twice, c)
+
+        def put(p, part, total):
+            twice[s, p, part] = total
+
+        neighbour_sum(once, around(once, c), [(p, p + 1) for p in range(5)], put)
+
+        @pl.when(jnp.logical_not(has_l))
+        def _():
+            clear(twice, s, range(0, 1))
+
+        @pl.when(jnp.logical_not(has_r))
+        def _():
+            clear(twice, s, range(4, 5))
+
+    def third_sum(c):
+        def put(p, part, total):
+            columns = slice(p * LANES, (p + 1) * LANES)
+            lines = pl.ds(3 * nz + part.start, ROWS)
+            head[lines, columns], tail[lines, columns] = halves(total)
+
+        neighbour_sum(twice, around(twice, c), [(p, p + 1) for p in range(3)], put)
+        for k, (source, s, first) in enumerate(
+            ((cells, c + 1, 2), (once, slot(once, c), 2), (twice, slot(twice, c), 1))
+        ):
+            lines = slice(k * nz, (k + 1) * nz)
+            for p in range(3):
+                columns = slice(p * LANES, (p + 1) * LANES)
+                head[lines, columns], tail[lines, columns] = halves(source[s, first + p])
+        product = product_of(terms, slice(0, 4 * nz), head[...], tail[...])
+        for p in range(3):
+            sums[slot(sums, c), p] = product[:, p * LANES : (p + 1) * LANES]
 
     def add_far(j):
-        source = stacked([far_l[j], far_r[j]])
-        product = jnp.dot(terms[3], source, preferred_element_type=F32)
-        s = slot(v0, j)
+        far = jnp.concatenate([far_l[j], far_r[j]], axis=1)
+        product = product_of(terms, slice(3 * nz, 4 * nz), *halves(far))
+        s = slot(sums, j)
         columns = cut(j)
         for p in range(3):
-            total = v0[s, p]
+            total = sums[s, p]
             if p == 0:
                 total = total + product[:, 0:LANES]
             if p == 2:
@@ -298,13 +345,6 @@
                 doubled[p, pl.ds(side, nz // 2, stride=2)] = total[nz:rows]
             pend[p, :, columns] = doubled[p]
 
-    def zero_slot(ring, c):
-        def body(p, _):
-            ring[slot(ring, c), p] = jnp.zeros((rows, LANES), F32)
-            return 0
-
-        lax.fori_loop(0, ring.shape[1], body, 0)
-
     def step(c, _):
         @pl.when(c < chunks)
         def _():
@@ -324,33 +364,25 @@
             for i in range(LAG):
                 start(far_left, far_right, chunks - LAG + i)
 
-        @pl.when(c < chunks)
-        def _():
-            spread_out(c)
-
-        @pl.when(c == chunks)
-        def _():
-            zero_slot(v3, chunks)
-
         @pl.when((c >= 1) & (c < chunks + 1))
         def _():
-            neighbours(v3, v2, 1, 2 * skip_l, 7 - 2 * skip_r, c - 1)
+            first_sum(c - 1)
 
         @pl.when(c == chunks + 1)
         def _():
-            zero_slot(v2, chunks)
+            clear(once, slot(once, chunks), range(7))
 
         @pl.when((c >= 2) & (c < chunks + 2))
         def _():
-            neighbours(v2, v1, 1, skip_l, 5 - skip_r, c - 2)
+            second_sum(c - 2)
 
         @pl.when(c == chunks + 2)
         def _():
-            zero_slot(v1, chunks)
+            clear(twice, slot(twice, chunks), range(5))
 
         @pl.when((c >= 3) & (c < chunks + 3))
         def _():
-            neighbours(v1, v0, 1, 0, 3, c - 3)
+            third_sum(c - 3)
 
         @pl.when(c >= LAG)
         def _():
@@ -393,15 +425,14 @@
             in_specs=[anywhere] * 5,
             out_specs=(vmem, vmem),
             scratch_shapes=[
-                pltpu.VMEM((chunks, planes, nz, LANES), F32),
-                pltpu.VMEM((chunks, 2, nz, LANES), F32),
-                pltpu.VMEM((chunks, 2, nz, LANES), F32),
+                pltpu.VMEM((chunks + 2, planes + 4, nz, LANES), F32),
                 pltpu.VMEM((chunks, nz, LANES), F32),
                 pltpu.VMEM((chunks, nz, LANES), F32),
-                pltpu.VMEM((3, planes + 6, rows, LANES), F32),
-                pltpu.VMEM((4, planes + 4, rows, LANES), F32),
-                pltpu.VMEM((5, planes + 2, rows, LANES), F32),
-                pltpu.VMEM((5, planes, rows, LANES), F32),
+                pltpu.VMEM((3, planes + 4, nz, LANES), F32),
+                pltpu.VMEM((3, planes + 2, nz, LANES), F32),
+                pltpu.VMEM((4 * nz, planes * LANES), BF16),
+                pltpu.VMEM((4 * nz, planes * LANES), BF16),
+                pltpu.VMEM((LAG - 2, planes, rows, LANES), F32),
                 pltpu.VMEM(fine.shape[1:], F32),
                 pltpu.VMEM(two.shape, F32),
                 pltpu.VMEM(three.shape, F32),
@@ -410,7 +441,7 @@
                 pltpu.VMEM((3, nz, nz), F32),
                 pltpu.VMEM((3 * nz, nz), F32),
                 pltpu.VMEM((4, rows, nz), F32),
-                pltpu.VMEM((4, rows, 3 * nz), BF16),
+                pltpu.VMEM((2 * rows, 4 * nz), BF16),
                 pltpu.VMEM((planes, nz, LANES), F32),
                 pltpu.VMEM((2, nz // 2, nz // 2), F32),
                 pltpu.VMEM((nz, nz // 2), F32),

time: 101 us -> 83.3 us (0.82)
  Pallas kernels: 101 us -> 82.3 us
    pallas_call x1, Pallas kernels: 95.9 us -> 77.6 us  [per_device(): pl.pallas_call(body, out_shape=(pltpu.VMEM(shape, F32), pltpu.VMEM(shape,...]
where the time goes in v1:
time: 83.3 us; the launch traced here: 82.9 us
  Pallas kernels  82.3 us (99%)
    pallas_call x1, Pallas kernels, per_device(): pl.pallas_call(body, out_shape=(pltpu.VMEM(shape, F32), pltpu.VMEM(shape,...  77.6 us
    pallas_call x1, Pallas kernels, per_device(): pl.pallas_call(put_out, out_shape=(jax.ShapeDtypeStruct(shape, F32), jax....  4.65 us

profile of v1, /device:TPU:31, one launch (start us, length us, event | category | flops | bytes accessed | tf_op | source)
XLA Modules:
  0.0 82.9 jit_solution(1694068266287748969)
XLA Ops:
  0.6 77.6 %shard_map.68 = (f32[3,256,2048]{2,1,0:T(8,128)S(1)}, f32[3,256,2048]{2,1,0:T(8,128)S(1)}) custom-call(f32[3,256,2048]{2,1,0:T(8,128)} %refs_0_.1, f32[1,256,256]{2,1,0:T(8,128)} %refs_1_.1, f32[128,128]{1,0:T(8,128)} %refs_2_.1, f32[64,64]{1,0:T(8,128)} %refs_3_.1, f32[32,32]{1,0:T(8,128)} %refs_4_.1), custom_call_target="tpu_custom_call" | custom-call | tf_op jit(solution)/shard_map/pallas_call | solution.py:422
  78.2 4.6 %shard_map.69 = (f32[3,256,2048]{2,1,0:T(8,128)}, f32[3,256,2048]{2,1,0:T(8,128)}) custom-call(f32[3,256,2048]{2,1,0:T(8,128)S(1)} %get-tuple-element.4.sol, f32[3,256,2048]{2,1,0:T(8,128)S(1)} %get-tuple-element.5.pend), custom_call_target="tpu_custom_call" | custom-call | tf_op jit(solution)/shard_map/pallas_call | solution.py:461

commit v2 on v1

--- a/solution.py
+++ b/solution.py
@@ -11,8 +11,8 @@
 
 FINE_Z = 4.0
 LANES = 128
-AHEAD = 3
-LAG = 6
+AHEAD = 6
+LAG = 12
 ROWS = 32
 
 

time: 83.3 us -> 81.9 us (0.983)
  Pallas kernels: 82.3 us -> 81.2 us
    pallas_call x1, Pallas kernels: 77.6 us -> 76.6 us  [per_device(): pl.pallas_call(body, out_shape=(pltpu.VMEM(shape, F32), pltpu.VMEM(shape,...]
where the time goes in v2:
time: 81.9 us; the launch traced here: 81.8 us
  Pallas kernels  81.2 us (99%)
    pallas_call x1, Pallas kernels, per_device(): pl.pallas_call(body, out_shape=(pltpu.VMEM(shape, F32), pltpu.VMEM(shape,...  76.6 us
    pallas_call x1, Pallas kernels, per_device(): pl.pallas_call(put_out, out_shape=(jax.ShapeDtypeStruct(shape, F32), jax....  4.65 us

profile of v2, /device:TPU:31, one launch (start us, length us, event | category | flops | bytes accessed | tf_op | source)
XLA Modules:
  0.0 81.8 jit_solution(3024567235706270302)
XLA Ops:
  0.6 76.6 %shard_map.68 = (f32[3,256,2048]{2,1,0:T(8,128)S(1)}, f32[3,256,2048]{2,1,0:T(8,128)S(1)}) custom-call(f32[3,256,2048]{2,1,0:T(8,128)} %refs_0_.1, f32[1,256,256]{2,1,0:T(8,128)} %refs_1_.1, f32[128,128]{1,0:T(8,128)} %refs_2_.1, f32[64,64]{1,0:T(8,128)} %refs_3_.1, f32[32,32]{1,0:T(8,128)} %refs_4_.1), custom_call_target="tpu_custom_call" | custom-call | tf_op jit(solution)/shard_map/pallas_call | solution.py:422
  77.2 4.6 %shard_map.69 = (f32[3,256,2048]{2,1,0:T(8,128)}, f32[3,256,2048]{2,1,0:T(8,128)}) custom-call(f32[3,256,2048]{2,1,0:T(8,128)S(1)} %get-tuple-element.4.sol, f32[3,256,2048]{2,1,0:T(8,128)S(1)} %get-tuple-element.5.pend), custom_call_target="tpu_custom_call" | custom-call | tf_op jit(solution)/shard_map/pallas_call | solution.py:461

commit v3 on v2

--- a/solution.py
+++ b/solution.py
@@ -150,12 +150,12 @@
 
     pl.semaphore_wait(barrier, has_l.astype(jnp.int32) + has_r.astype(jnp.int32))
 
-    def cut(c):
-        return pl.ds(pl.multiple_of(c * LANES, LANES), LANES)
-
-    def remote(planes, target, sends, recvs, way, c, device):
+    def cut(c, lanes=LANES):
+        return pl.ds(pl.multiple_of(c * lanes, lanes), lanes)
+
+    def remote(planes, target, sends, recvs, way, c, device, lanes=LANES):
         return pltpu.make_async_remote_copy(
-            src_ref=right_side.at[planes, :, cut(c)],
+            src_ref=right_side.at[planes, :, cut(c, lanes)],
             dst_ref=target,
             send_sem=sends.at[way, c],
             recv_sem=recvs.at[way, c],
@@ -163,13 +163,13 @@
             device_id_type=MESH,
         )
 
-    def near_left(c):
-        target = cells.at[c + 1, pl.ds(5, 2)]
-        return remote(pl.ds(0, 2), target, near_send, near_recv, 0, c, me - 1)
-
-    def near_right(c):
-        target = cells.at[c + 1, pl.ds(0, 2)]
-        return remote(pl.ds(1, 2), target, near_send, near_recv, 1, c, me + 1)
+    def near_left(u):
+        target = cells.at[u + 1, pl.ds(5, 2)]
+        return remote(pl.ds(0, 2), target, near_send, near_recv, 0, u, me - 1, 2 * LANES)
+
+    def near_right(u):
+        target = cells.at[u + 1, pl.ds(0, 2)]
+        return remote(pl.ds(1, 2), target, near_send, near_recv, 1, u, me + 1, 2 * LANES)
 
     def far_left(c):
         return remote(2, far_r.at[c], far_send, far_recv, 0, c, me - 1)
@@ -197,8 +197,8 @@
             to_right(c).wait_send()
             to_left(c).wait_recv()
 
-    for c in range(AHEAD):
-        start(near_left, near_right, c)
+    for u in range(AHEAD // 2):
+        start(near_left, near_right, u)
 
     small = [
         pltpu.make_async_copy(src, dst, small_sem.at[i])
@@ -209,17 +209,17 @@
     for copy in small:
         copy.start()
 
-    def own_copy(c):
+    def own_copy(u):
         return pltpu.make_async_copy(
-            right_side.at[:, :, cut(c)], cells.at[c + 1, pl.ds(2, 3)], own_sem.at[c]
+            right_side.at[:, :, cut(u, 2 * LANES)], cells.at[u + 1, pl.ds(2, 3)], own_sem.at[u]
         )
 
-    lax.fori_loop(0, chunks, lambda c, _: (own_copy(c).start(), 0)[1], 0)
+    lax.fori_loop(0, chunks // 2, lambda u, _: (own_copy(u).start(), 0)[1], 0)
 
     plane = jnp.zeros((nz, LANES), F32)
     for p in range(7):
-        cells[0, p] = plane
-        cells[chunks + 1, p] = plane
+        cells[0, p, :, LANES:] = plane
+        cells[chunks // 2 + 1, p, :, 0:LANES] = plane
 
     def clear(ring, s, planes):
         for p in planes:
@@ -231,7 +231,8 @@
     @pl.when(jnp.logical_not(has_l))
     def _():
         def body(c, _):
-            clear(cells, c + 1, range(0, 2))
+            for p in range(0, 2):
+                cells[1 + c // 2, p, :, cut(lax.rem(c, 2))] = plane
             far_l[c] = plane
             return 0
 
@@ -240,7 +241,8 @@
     @pl.when(jnp.logical_not(has_r))
     def _():
         def body(c, _):
-            clear(cells, c + 1, range(5, 7))
+            for p in range(5, 7):
+                cells[1 + c // 2, p, :, cut(lax.rem(c, 2))] = plane
             far_r[c] = plane
             return 0
 
@@ -261,14 +263,14 @@
     lane = lax.broadcasted_iota(jnp.int32, (ROWS, LANES), 1)
     first_lane, last_lane = lane == 0, lane == LANES - 1
 
-    def neighbour_sum(source, slots, targets, put):
-        before, here, after = slots
+    def neighbour_sum(count_of, views, targets, put):
+        before, here, after = views
         for b in range(nz // ROWS):
             part = pl.ds(b * ROWS, ROWS)
-            centres = [source[here, q, part] for q in range(source.shape[1])]
+            centres = [here(q, part) for q in range(count_of)]
             for p, q in targets:
-                up = jnp.where(first_lane, source[after, q, part], centres[q])
-                down = jnp.where(last_lane, source[before, q, part], centres[q])
+                up = jnp.where(first_lane, after(q, part), centres[q])
+                down = jnp.where(last_lane, before(q, part), centres[q])
                 total = pltpu.roll(up, LANES - 1, 1) + pltpu.roll(down, 1, 1)
                 for x in (q - 1, q + 1):
                     if 0 <= x < len(centres):
@@ -277,7 +279,12 @@
 
     def around(ring, c):
         size = ring.shape[0]
-        return tuple(lax.rem(c + size + i, size) for i in (-1, 0, 1))
+        slots = [lax.rem(c + size + i, size) for i in (-1, 0, 1)]
+        return [lambda q, part, s=s: ring[s, q, part] for s in slots]
+
+    def cells_at(c):
+        u, columns = lax.div(c + 2, 2), cut(lax.rem(c + 2, 2))
+        return lambda q, part: cells[u, q, part, columns]
 
     def first_sum(c):
         s = slot(once, c)
@@ -285,7 +292,7 @@
         def put(p, part, total):
             once[s, p, part] = total
 
-        neighbour_sum(cells, (c, c + 1, c + 2), [(p, p) for p in range(7)], put)
+        neighbour_sum(7, [cells_at(c + i) for i in (-1, 0, 1)], [(p, p) for p in range(7)], put)
 
         @pl.when(jnp.logical_not(has_l))
         def _():
@@ -301,7 +308,7 @@
         def put(p, part, total):
             twice[s, p, part] = total
 
-        neighbour_sum(once, around(once, c), [(p, p + 1) for p in range(5)], put)
+        neighbour_sum(7, around(once, c), [(p, p + 1) for p in range(5)], put)
 
         @pl.when(jnp.logical_not(has_l))
         def _():
@@ -317,14 +324,13 @@
             lines = pl.ds(3 * nz + part.start, ROWS)
             head[lines, columns], tail[lines, columns] = halves(total)
 
-        neighbour_sum(twice, around(twice, c), [(p, p + 1) for p in range(3)], put)
-        for k, (source, s, first) in enumerate(
-            ((cells, c + 1, 2), (once, slot(once, c), 2), (twice, slot(twice, c), 1))
-        ):
+        neighbour_sum(5, around(twice, c), [(p, p + 1) for p in range(3)], put)
+        views = ((cells_at(c), 2), (around(once, c)[1], 2), (around(twice, c)[1], 1))
+        for k, (view, first) in enumerate(views):
             lines = slice(k * nz, (k + 1) * nz)
             for p in range(3):
                 columns = slice(p * LANES, (p + 1) * LANES)
-                head[lines, columns], tail[lines, columns] = halves(source[s, first + p])
+                head[lines, columns], tail[lines, columns] = halves(view(first + p, pl.ds(0, nz)))
         product = product_of(terms, slice(0, 4 * nz), head[...], tail[...])
         for p in range(3):
             sums[slot(sums, c), p] = product[:, p * LANES : (p + 1) * LANES]
@@ -346,18 +352,21 @@
             pend[p, :, columns] = doubled[p]
 
     def step(c, _):
-        @pl.when(c < chunks)
-        def _():
-            own_copy(c).wait()
-            finish(near_left, near_right, c)
-
-        @pl.when(c + AHEAD < chunks)
-        def _():
-            start(near_left, near_right, c + AHEAD)
-
-            @pl.when(c + AHEAD >= LAG)
-            def _():
-                start(far_left, far_right, c + AHEAD - LAG)
+        pair = lax.div(c, 2)
+        is_even = lax.rem(c, 2) == 0
+
+        @pl.when(is_even & (c < chunks))
+        def _():
+            own_copy(pair).wait()
+            finish(near_left, near_right, pair)
+
+        @pl.when(is_even & (c + AHEAD < chunks))
+        def _():
+            start(near_left, near_right, pair + AHEAD // 2)
+
+        @pl.when((c + AHEAD < chunks) & (c + AHEAD >= LAG))
+        def _():
+            start(far_left, far_right, c + AHEAD - LAG)
 
         @pl.when(c + AHEAD == chunks)
         def _():
@@ -425,7 +434,7 @@
             in_specs=[anywhere] * 5,
             out_specs=(vmem, vmem),
             scratch_shapes=[
-                pltpu.VMEM((chunks + 2, planes + 4, nz, LANES), F32),
+                pltpu.VMEM((chunks // 2 + 2, planes + 4, nz, 2 * LANES), F32),
                 pltpu.VMEM((chunks, nz, LANES), F32),
                 pltpu.VMEM((chunks, nz, LANES), F32),
                 pltpu.VMEM((3, planes + 4, nz, LANES), F32),
@@ -445,7 +454,7 @@
                 pltpu.VMEM((planes, nz, LANES), F32),
                 pltpu.VMEM((2, nz // 2, nz // 2), F32),
                 pltpu.VMEM((nz, nz // 2), F32),
-                pltpu.SemaphoreType.DMA((chunks,)),
+                pltpu.SemaphoreType.DMA((chunks // 2,)),
                 pltpu.SemaphoreType.DMA((4,)),
                 pltpu.SemaphoreType.DMA((2, chunks)),
                 pltpu.SemaphoreType.DMA((2, chunks)),

time: 81.9 us -> 81.9 us (level)
  no operation moved by 1% of the time
where the time goes in v3:
time: 81.9 us; the launch traced here: 81.8 us
  Pallas kernels  81.1 us (99%)
    pallas_call x1, Pallas kernels, per_device(): pl.pallas_call(body, out_shape=(pltpu.VMEM(shape, F32), pltpu.VMEM(shape,...  76.5 us
    pallas_call x1, Pallas kernels, per_device(): pl.pallas_call(put_out, out_shape=(jax.ShapeDtypeStruct(shape, F32), jax....  4.65 us

profile of v3, /device:TPU:31, one launch (start us, length us, event | category | flops | bytes accessed | tf_op | source)
XLA Modules:
  0.0 81.8 jit_solution(6046112689953026634)
XLA Ops:
  0.6 76.5 %shard_map.68 = (f32[3,256,2048]{2,1,0:T(8,128)S(1)}, f32[3,256,2048]{2,1,0:T(8,128)S(1)}) custom-call(f32[3,256,2048]{2,1,0:T(8,128)} %refs_0_.1, f32[1,256,256]{2,1,0:T(8,128)} %refs_1_.1, f32[128,128]{1,0:T(8,128)} %refs_2_.1, f32[64,64]{1,0:T(8,128)} %refs_3_.1, f32[32,32]{1,0:T(8,128)} %refs_4_.1), custom_call_target="tpu_custom_call" | custom-call | tf_op jit(solution)/shard_map/pallas_call | solution.py:431
  77.1 4.6 %shard_map.69 = (f32[3,256,2048]{2,1,0:T(8,128)}, f32[3,256,2048]{2,1,0:T(8,128)}) custom-call(f32[3,256,2048]{2,1,0:T(8,128)S(1)} %get-tuple-element.4.sol, f32[3,256,2048]{2,1,0:T(8,128)S(1)} %get-tuple-element.5.pend), custom_call_target="tpu_custom_call" | custom-call | tf_op jit(solution)/shard_map/pallas_call | solution.py:470
